TPU v7x, 128 devices: a whole 4x4x4 slice. The times are simulated.
128 devices in a mesh: seq: 4 (over z), head: 32 (over y, x, core).
Axes of the slice: x: 4, y: 4, z: 4, core: 2. Of those that a mesh axis runs over, the one named last changes fastest.
Arguments:
- queries: float32 [8192, 4096], P('seq', 'head'), may hold values from -6 to 6
- key_rows: float32 [8192, 4096], P('seq', 'head'), may hold values from -6 to 6
- values: float32 [8192, 4096], P('seq', 'head'), may hold values from -6 to 6
- out_weight: bfloat16 [4096, 2048], P('head'), may hold values from -0.09375 to 0.09375
- expert_ids: int32 [8192, 8], P(('seq', 'head')), may hold values from 0 to 127, all different within a row; in each aligned block of 64 rows (0 to 63, 64 to 127, ...) at most 8 rows name the same one
- gate_ints: int32 [8192, 8], P(('seq', 'head')), may hold values from 1 to 1023
- w_gate: bfloat16 [128, 2048, 768], P(('seq', 'head')), may hold values from -0.125 to 0.125
- w_up: bfloat16 [128, 2048, 768], P(('seq', 'head')), may hold values from -0.125 to 0.125
- w_down: bfloat16 [128, 768, 2048], P(('seq', 'head')), may hold values from -0.21875 to 0.21875
Outputs:
- layer_out: float32 [8192, 2048], P(('seq', 'head'))
Inputs may be any that keep to these rules, and one draw needn't show every extreme that they name: `expert_ids`: each row names 8 different experts. Within the rows of one device (aligned blocks of 64 rows) no expert is named more than 8 times, a bound that some block reaches.
All inputs are finite; a program needn't handle non-finite values.
Results may differ from a plain program's by a relative error of at most 0.017.
Values may be sent and summed in bfloat16 or wider, within the bound.
A program may use at most 128 MiB of HBM per device.

v0:
```python
import math
import jax
import jax.numpy as jnp
from jax import lax
from jax.sharding import PartitionSpec as P

DH = 128
HIGH = lax.Precision.HIGHEST


def cut_along(array, dim, devices):
    dims = array.shape
    blocks = array.reshape(*dims[:dim], devices, dims[dim] // devices, *dims[dim + 1 :])
    return jnp.moveaxis(blocks, dim, 0)


def laid_out(blocks, dim):
    blocks = jnp.moveaxis(blocks, 0, dim)
    dims = blocks.shape
    return blocks.reshape(*dims[:dim], dims[dim] * dims[dim + 1], *dims[dim + 2 :])


def exchange_both(array, axis, axes, splits, concats):
    sizes = [lax.axis_size(a) for a in axes]
    blocks = cut_along(array, splits[0], sizes[0])
    blocks = jnp.moveaxis(cut_along(blocks, splits[1] + 1, sizes[1]), 0, 1)
    inside = blocks.shape[2:]
    blocks = blocks.reshape(-1, *inside)
    blocks = lax.all_to_all(blocks, axis, split_axis=0, concat_axis=0, tiled=True)
    blocks = laid_out(blocks.reshape(*sizes, *inside), concats[0] + 1)
    return laid_out(blocks, concats[1])


def causal_linear(query_heads, key_heads, value_heads):
    heads, length, width = query_heads.shape
    block = math.gcd(512, length)
    count = length // block

    def split(array):
        return array.reshape(heads, count, block, width).transpose(1, 0, 2, 3)

    lower = jnp.tril(jnp.ones((block, block), jnp.float32))

    def advance(state, inputs):
        query_block, key_block, value_block = inputs
        scores = jnp.einsum("hid,hjd->hij", query_block, key_block, precision=HIGH) * lower
        output = jnp.einsum("hij,hjd->hid", scores, value_block, precision=HIGH)
        output = output + jnp.einsum("hid,hde->hie", query_block, state, precision=HIGH)
        state = state + jnp.einsum("hjd,hje->hde", key_block, value_block, precision=HIGH)
        return (state, output)

    start = jnp.zeros((heads, width, width), jnp.float32)
    state, outputs = lax.scan(
        advance, start, (split(query_heads), split(key_heads), split(value_heads))
    )
    return (outputs.transpose(1, 0, 2, 3).reshape(heads, length, width), state)


def shards(queries, key_rows, values, out_weight, expert_ids, gate_ints, w_gate, w_up, w_down):
    length = queries.shape[0]
    heads_here = queries.shape[1] // DH

    def split_heads(array):
        return array.reshape(length, heads_here, DH).transpose(1, 0, 2)

    query_heads = split_heads(queries)
    local_out, local_state = causal_linear(query_heads, split_heads(key_rows), split_heads(values))
    every_state = lax.all_gather(
        local_state[None].astype(jnp.bfloat16), "seq", axis=0, tiled=True
    ).astype(jnp.float32)
    before = (jnp.arange(every_state.shape[0], dtype=jnp.int32) < lax.axis_index("seq")).astype(
        jnp.float32
    )
    earlier = jnp.sum(every_state * before[:, None, None, None], axis=0)
    heads_out = local_out + jnp.einsum("hid,hde->hie", query_heads, earlier, precision=HIGH)
    heads_out = heads_out * lax.rsqrt(
        jnp.mean(heads_out * heads_out, axis=-1, keepdims=True) + 1e-06
    )
    attn = heads_out.transpose(1, 0, 2).reshape(length, heads_here * DH).astype(jnp.bfloat16)
    head_count = lax.axis_size("head")
    seq_count = lax.axis_size("seq")
    tok_count = length // head_count
    all_heads = lax.all_to_all(attn, "head", split_axis=0, concat_axis=1, tiled=True)
    all_rows = lax.all_gather(out_weight, "head", axis=0, tiled=True)
    projected = jnp.dot(all_heads, all_rows, preferred_element_type=jnp.float32)
    normed = (
        projected * lax.rsqrt(jnp.mean(projected * projected, axis=-1, keepdims=True) + 1e-06)
    ).astype(jnp.bfloat16)
    gates = gate_ints.astype(jnp.float32)
    gates = gates / jnp.sum(gates, axis=-1, keepdims=True)
    top_count = expert_ids.shape[1]
    local_experts = w_gate.shape[0]
    devices = seq_count * head_count
    experts = local_experts * devices
    capacity = max(2, 2 * tok_count * top_count // experts)
    width = normed.shape[1]
    flat_ids = expert_ids.reshape(-1)
    assigned = flat_ids.shape[0]
    onehot = (flat_ids[:, None] == jnp.arange(experts, dtype=jnp.int32)[None, :]).astype(jnp.int32)
    before_count = jnp.cumsum(onehot, axis=0, dtype=jnp.int32) - onehot
    position = jnp.sum(before_count * onehot, axis=1, dtype=jnp.int32)
    slot_index = flat_ids * capacity + position
    source = (
        jnp.zeros((experts * capacity,), jnp.int32)
        .at[slot_index]
        .set(jnp.arange(assigned, dtype=jnp.int32))
    )
    filled = jnp.zeros((experts * capacity,), jnp.bool_).at[slot_index].set(True)
    picked = normed[source // top_count]
    outgoing = jnp.where(filled[:, None], picked, jnp.zeros_like(picked))
    outgoing = outgoing.reshape(seq_count, head_count, local_experts, capacity, width)
    received = exchange_both(outgoing, ("seq", "head"), ("seq", "head"), (0, 1), (0, 1))
    expert_received = received.reshape(devices, local_experts, capacity, width)
    gate_val = jnp.einsum(
        "nesd,edf->nesf", expert_received, w_gate, preferred_element_type=jnp.float32
    )
    up_val = jnp.einsum("nesd,edf->nesf", expert_received, w_up, preferred_element_type=jnp.float32)
    act = (jax.nn.silu(gate_val) * up_val).astype(jnp.bfloat16)
    result = jnp.einsum("nesf,efd->nesd", act, w_down, preferred_element_type=jnp.float32).astype(
        jnp.bfloat16
    )
    result = result.reshape(seq_count, head_count, local_experts, capacity, width)
    returned = exchange_both(result, ("seq", "head"), ("seq", "head"), (0, 1), (0, 1))
    returned = returned.reshape(experts * capacity, width)
    gathered = returned[slot_index].astype(jnp.float32) * gates.reshape(-1)[:, None]
    mixture = jnp.sum(gathered.reshape(tok_count, top_count, width), axis=1)
    return projected + mixture


def solution(mesh):
    placed = (
        P("seq", "head"),
        P("seq", "head"),
        P("seq", "head"),
        P("head", None),
        P(("seq", "head"), None),
        P(("seq", "head"), None),
        P(("seq", "head"), None, None),
        P(("seq", "head"), None, None),
        P(("seq", "head"), None, None),
    )
    return jax.shard_map(
        shards, mesh=mesh, in_specs=placed, out_specs=P(("seq", "head"), None), check_vma=False
    )
```

profile of v0, /device:TPU:1, one launch (start us, length us, event | category | flops | bytes accessed | tf_op | source)
XLA Modules:
  0.0 276.8 jit_solution(5523111241887061232)
XLA Ops:
  6.5 0.0 copy-start
  6.5 0.0 all-gather.3.cloned.1.call-start
  6.5 0.7 all-gather.3.cloned.1.call-update
  7.3 30.9 %while.13 = (s32[]{:T(128)}, f32[1,128,128]{2,1,0:T(8,128)S(1)}, f32[4,1,512,128]{3,2,1,0:T(8,128)}, f32[4,1,512,128]{3,2,1,0:T(8,128)}, f32[4,1,512,128]{3,2,1,...) while((s32[]{:T(128)}, f32[1,128,128]{2,1,0:T(8,128)S(1)}, ...), condition=%wide.region_1.2_spmd.clone, body=%wide.region_0.1_spmd.clone.sunk | while | flops 1007534080 | bytes 4656736 | solution.py:53
  7.3 2.2 convolution_multiply_fusion.2
  9.5 1.9 fusion.89
  11.5 2.0 fusion.90
  13.5 1.6 fusion.88
  15.1 2.0 convolution_multiply_fusion.2
  17.1 1.9 fusion.89
  19.1 2.0 fusion.90
  21.1 1.6 fusion.88
  22.8 2.1 convolution_multiply_fusion.2
  24.8 1.9 fusion.89
  26.8 2.0 fusion.90
  28.8 1.6 fusion.88
  30.5 2.0 convolution_multiply_fusion.2
  32.5 1.9 fusion.89
  34.5 2.0 fusion.90
  36.5 1.6 fusion.88
  38.2 2.6 copy.37
  40.8 12.0 %all-gather = bf16[4,128,128]{2,1,0:T(8,128)(2,1)S(1)} all-gather(bf16[1,128,128]{2,1,0:T(8,128)(2,1)S(1)} %convert_element_type.66), channel_id=2, replica_groups=mesh['seq'=4,'head'=32] {'seq'}, dimensions={0}, use_global_device_ids=true | all-gather | bytes 163840 | tf_op jit(solution)/shard_map/all_gather | solution.py:68
  52.7 0.1 fusion.50
  52.8 0.0 copy-start.3
  52.8 2.7 multiply_reduce_fusion
  55.6 0.9 multiply_convert_fusion
  56.5 2.1 copy.26
  58.6 9.8 %all-to-all-start = ((bf16[32,64,128]{2,1,0:T(8,128)(2,1)}), bf16[32,64,128]{2,1,0:T(8,128)(2,1)}, u32[]{:S(2)}, u32[]{:S(2)}) async-start(bf16[32,64,128]{2,1,0:T(8,128)(2,1)} %bitcast.182), calls=%async_computation | async-start | bytes 1048576 | tf_op jit(solution)/shard_map/all_to_all | solution.py:83
  68.3 0.0 copy-done.3
  68.3 0.1 copy.29
  68.4 0.1 eq.29
  68.5 0.1 eq.25
  68.6 0.1 copy.31
  68.7 0.2 fusion.51
  69.0 0.2 fusion.49
  69.3 0.1 copy.28
  69.4 0.1 mul.78
  69.5 2.4 scatter_custom_fusion.1
  71.9 2.6 scatter_custom_fusion
  74.6 0.1 broadcast_in_dim.56
  74.7 9.7 %all-to-all-done = bf16[32,64,128]{2,1,0:T(8,128)(2,1)} async-done(((bf16[32,64,128]{2,1,0:T(8,128)(2,1)}), bf16[32,64,128]{2,1,0:T(8,128)(2,1)}, u32[]{:S(2)}, u32[]{:S(2)}) %all-to-all-start) | async-done | bytes 524320 | tf_op jit(solution)/shard_map/all_to_all | solution.py:83
  84.4 6.9 %all-gather.3.cloned.1.call-done = bf16[4096,2048]{1,0:T(8,128)(2,1)} async-done(((bf16[128,2048]{1,0:T(8,128)(2,1)}), bf16[4096,2048]{1,0:T(8,128)(2,1)}) %all-gather.3.cloned.1.call-update) | async-done | bytes 16777232 | tf_op jit(solution)/shard_map/all_gather | solution.py:84
  91.3 9.1 %multiply_reduce_fusion.1 = (f32[64]{0:T(128)S(1)}, f32[64,2048]{1,0:T(8,128)S(1)}) fusion(bf16[4096,2048]{1,0:T(8,128)(2,1)} %all-gather.3.cloned.1.call-done, bf16[32,64,128]{2,1,0:T(8,128)(2,1)} %all-to-all-done), kind=kOutput, calls=%fused_computation.59 | convolution fusion | flops 1074003968 | bytes 17826048 | tf_op jit(solution)/shard_map/dot_general | solution.py:85
  100.3 0.0 copy-start.1
  100.4 0.8 copy-done.1
  101.1 0.1 multiply_convert_fusion.1
  101.2 6.0 %gather_fusion = bf16[1024,2048]{1,0:T(8,128)(2,1)} fusion(bf16[64,2048]{1,0:T(8,128)(2,1)S(1)} %multiply_convert_fusion.1, s32[1024]{0:T(1024)S(1)} %fusion.55), kind=kCustom, calls=%fused_computation | custom fusion | bytes 8392704 | tf_op jit(solution)/shard_map/gather | solution.py:109
  107.3 2.5 bitcast_select_fusion
  109.8 60.2 %all_to_all.26 = bf16[128,1,1,1,8,2048]{5,4,3,2,1,0:T(8,128)(2,1)S(1)} all-to-all(bf16[128,1,1,1,8,2048]{5,4,3,2,1,0:T(8,128)(2,1)S(1)} %bitcast_select_fusion), channel_id=1, replica_groups=mesh['seq'=4,'head'=32] {'seq','head'}, dimensions={0} | all-to-all | bytes 8388608 | tf_op jit(solution)/shard_map/all_to_all | solution.py:29
  170.0 2.3 copy.34
  172.3 0.0 copy-start.2
  172.3 2.0 copy-done.2
  174.3 0.0 copy-done.5
  174.3 5.2 %fusion.30 = f32[128,8,768]{2,0,1:T(8,128)} fusion(bf16[128,8,2048]{2,0,1:T(8,128)(2,1)S(1)} %bitcast.180, bf16[1,2048,768]{2,1,0:T(8,128)(2,1)S(1)} %copy-done.5), kind=kOutput, calls=%fused_computation.41 | convolution fusion | flops 3221225472 | bytes 10485760 | tf_op jit(solution)/shard_map/nesd,edf->nesf/dot_general | solution.py:117
  179.5 0.0 copy-done
  179.5 12.3 %convert_bitcast_fusion = bf16[128,1,1,1,8,2048]{5,0,4,3,2,1:T(8,128)(2,1)} fusion(bf16[1,768,2048]{2,1,0:T(8,128)(2,1)S(1)} %copy-done, f32[128,8,768]{2,0,1:T(8,128)} %fusion.30, bf16[128,8,2048]{2,0,1:T(8,128)(2,1)} %bitcast.181, bf16[1,2048,768]{2,1,0:T(8,128)(2,1)} %param.17), kind=kOutput, calls=%fused_computation.37 | convolution fusion | flops 6449266688 | bytes 17825792 | tf_op jit(solution)/shard_map/nesf,efd->nesd/dot_general | solution.py:119
  191.8 6.5 %copy.35 = bf16[128,1,1,1,8,2048]{5,4,3,2,1,0:T(8,128)(2,1)} copy(bf16[128,1,1,1,8,2048]{5,0,4,3,2,1:T(8,128)(2,1)} %convert_bitcast_fusion) | data formatting | bytes 8388608 | tf_op jit(solution)/shard_map/reshape;transpose;transpose;reshape;reshape;reshape | solution.py:28
  198.3 5.6 %all-to-all-start.2 = ((bf16[128,1,1,1,8,2048]{5,4,3,2,1,0:T(8,128)(2,1)}), bf16[128,1,1,1,8,2048]{5,4,3,2,1,0:T(8,128)(2,1)}, u32[]{:S(2)}, u32[]{:S(2)}) async-start(bf16[128,1,1,1,8,2048]{5,4,3,2,1,0:T(8,128)(2,1)} %copy.35), calls=%async_computation.2 | async-start | bytes 8388608 | tf_op jit(solution)/shard_map/all_to_all | solution.py:29
  203.9 0.0 copy-done.4
  203.9 0.1 copy.36
  204.0 52.6 %all-to-all-done.2 = bf16[128,1,1,1,8,2048]{5,4,3,2,1,0:T(8,128)(2,1)} async-done(((bf16[128,1,1,1,8,2048]{5,4,3,2,1,0:T(8,128)(2,1)}), bf16[128,1,1,1,8,2048]{5,4,3,2,1,0:T(8,128)(2,1)}, u32[]{:S(2)}, u32[]{:S(2)}) %all-to-all-start.2) | async-done | bytes 4194336 | tf_op jit(solution)/shard_map/all_to_all | solution.py:29
  256.6 8.0 %gather_fusion.1 = bf16[512,2048]{1,0:T(8,128)(2,1)} fusion(bf16[1024,2048]{1,0:T(8,128)(2,1)} %bitcast.46, s32[1024]{0:T(1024)S(1)} %pad_clamp_fusion), kind=kCustom, calls=%fused_computation.1 | custom fusion | bytes 4196352 | tf_op jit(solution)/shard_map/gather | solution.py:125
  264.6 3.4 %fusion.27 = f32[64,2048]{1,0:T(8,128)S(1)} fusion(bf16[512,2048]{1,0:T(8,128)(2,1)} %gather_fusion.1, f32[64,8]{1,0:T(8,128)S(1)} %copy.36), kind=kLoop, calls=%fused_computation.35 | loop fusion | flops 3014656 | bytes 2623488 | tf_op jit(solution)/shard_map/reduce_sum | solution.py:126
  268.1 1.9 add.82
  (22 shorter events, 0.2 us)
Async XLA Ops:
  6.5 172.9 %copy-start = (bf16[1,768,2048]{2,1,0:T(8,128)(2,1)S(1)}, bf16[1,768,2048]{2,1,0:T(8,128)(2,1)}, u32[]{:S(2)}) copy-start(bf16[1,768,2048]{2,1,0:T(8,128)(2,1)} %param.19) | copy-start | bytes 9437188
  6.5 84.7 %all-gather.3.cloned.1.call-start = ((), (), s32[]{:S(2)}) async-start(), calls=%async_computation.3 | async-start | bytes 17301504 | tf_op jit(solution)/shard_map/all_gather | solution.py:84
  52.8 15.5 %copy-start.3 = (s32[64,8]{0,1:T(8,128)S(1)}, s32[64,8]{0,1:T(8,128)}, u32[]{:S(2)}) copy-start(s32[64,8]{0,1:T(8,128)} %param.15) | copy-start | bytes 6148
  58.6 25.8 %all-to-all-start = ((bf16[32,64,128]{2,1,0:T(8,128)(2,1)}), bf16[32,64,128]{2,1,0:T(8,128)(2,1)}, u32[]{:S(2)}, u32[]{:S(2)}) async-start(bf16[32,64,128]{2,1,0:T(8,128)(2,1)} %bitcast.182), calls=%async_computation | async-start | bytes 1048576 | tf_op jit(solution)/shard_map/all_to_all | solution.py:83
  100.3 0.8 copy-start.1
  170.0 4.3 %copy-start.5 = (bf16[1,2048,768]{2,1,0:T(8,128)(2,1)S(1)}, bf16[1,2048,768]{2,1,0:T(8,128)(2,1)}, u32[]{:S(2)}) copy-start(bf16[1,2048,768]{2,1,0:T(8,128)(2,1)} %param.18) | copy-start | bytes 9437188
  172.3 2.0 copy-start.2
  198.2 5.6 %copy-start.4 = (s32[64,8]{0,1:T(8,128)S(1)}, s32[64,8]{0,1:T(8,128)}, u32[]{:S(2)}) copy-start(s32[64,8]{0,1:T(8,128)} %param.16) | copy-start | bytes 6148
  198.3 58.4 %all-to-all-start.2 = ((bf16[128,1,1,1,8,2048]{5,4,3,2,1,0:T(8,128)(2,1)}), bf16[128,1,1,1,8,2048]{5,4,3,2,1,0:T(8,128)(2,1)}, u32[]{:S(2)}, u32[]{:S(2)}) async-start(bf16[128,1,1,1,8,2048]{5,4,3,2,1,0:T(8,128)(2,1)} %copy.35), calls=%async_computation.2 | async-start | bytes 8388608 | tf_op jit(solution)/shard_map/all_to_all | solution.py:29
Sparse Core Ops, SparseCore 0:
  9.6 81.5 all-gather.2
where the time goes:
time: 278 us; the launch traced here: 277 us
  blocking collectives  72.2 us (26%)
  waiting for transfers between devices  69.9 us (25%)
  matrix products  60 us (22%)
  local copies, waits for them, and re-layouts  36.1 us (13%)
  starting transfers between devices  15.4 us (6%)
  between operations  13.6 us (5%)
  other arithmetic  9.54 us (3%)
    all_to_all x1, blocking collectives, exchange_both(): lax.all_to_all(blocks, axis, split_axis=0, concat_axis=0, tiled=True)  60.2 us
    all_to_all x1, waiting for transfers between devices, exchange_both(): lax.all_to_all(blocks, axis, split_axis=0, concat_axis=0, tiled=True)  52.6 us
    dot_general x1, matrix products, shards(): jnp.einsum('nesf,efd->nesd', act, w_down, preferred_element_type=jnp.floa...  12.3 us
    all_gather x1, blocking collectives, shards(): lax.all_gather(local_state[None].astype(jnp.bfloat16), 'seq', axis=0, til...  12 us
    all_to_all x1, starting transfers between devices, shards(): lax.all_to_all(attn, 'head', split_axis=0, concat_axis=1, tiled=True)  9.76 us
    all_to_all x1, waiting for transfers between devices, shards(): lax.all_to_all(attn, 'head', split_axis=0, concat_axis=1, tiled=True)  9.66 us
    dot_general x1, matrix products, shards(): projected = jnp.dot(all_heads, all_rows, preferred_element_type=jnp.float32)  9.08 us
    dot_general x4, matrix products, advance(): jnp.einsum('hid,hjd->hij', query_block, key_block, precision=HIGH) * lower  8.3 us
  transfers between devices with their start and end apart: 3, of which 3 were waited for; matrix products, arithmetic and copies ran while one was open for 16% of the time, Pallas kernels for 0%

commit v1 on v0

--- a/solution.py
+++ b/solution.py
@@ -6,6 +6,19 @@
 
 DH = 128
 HIGH = lax.Precision.HIGHEST
+
+
+def collect(x, axis, dim):
+    ways = lax.axis_size(axis)
+    up = [(d, (d + 1) % ways) for d in range(ways)]
+    down = [(d, (d - 1) % ways) for d in range(ways)]
+    earlier, later = ([x], [x])
+    for _ in range(ways // 2):
+        earlier.append(lax.ppermute(earlier[-1], axis, up))
+    for _ in range((ways - 1) // 2):
+        later.append(lax.ppermute(later[-1], axis, down))
+    line = jnp.concatenate([*earlier[::-1], *later[1:]], axis=dim)
+    return jnp.roll(line, (lax.axis_index(axis) - ways // 2) * x.shape[dim], axis=dim)
 
 
 def cut_along(array, dim, devices):
@@ -65,9 +78,7 @@
 
     query_heads = split_heads(queries)
     local_out, local_state = causal_linear(query_heads, split_heads(key_rows), split_heads(values))
-    every_state = lax.all_gather(
-        local_state[None].astype(jnp.bfloat16), "seq", axis=0, tiled=True
-    ).astype(jnp.float32)
+    every_state = collect(local_state[None].astype(jnp.bfloat16), "seq", 0).astype(jnp.float32)
     before = (jnp.arange(every_state.shape[0], dtype=jnp.int32) < lax.axis_index("seq")).astype(
         jnp.float32
     )

time: 278 us -> 278 us (level)
  blocking collectives: 72.2 us -> 60.2 us
  local copies, waits for them, and re-layouts: 36.1 us -> 41 us
  starting transfers between devices: 15.4 us -> 19.2 us
    all_gather x1 -> x0, blocking collectives: 12 us -> none  [shards(): lax.all_gather(local_state[None].astype(jnp.bfloat16), 'seq', axis=0, til...]
    ppermute x0 -> x3, starting transfers between devices: none -> 4.57 us  [the longest x2 2.54 us: collect(): earlier.append(lax.ppermute(earlier[-1], axis, up))]
    unnamed x14 -> x19, local copies, waits for them, and re-layouts: 2.85 us -> 5.92 us
  transfers between devices with their start and end apart: 3 -> 6, of which waited for: 3 -> 4; matrix products, arithmetic and copies ran while one was open for 16% -> 19% of each run, Pallas kernels for 0% -> 0%
where the time goes in v1:
time: 278 us; the launch traced here: 277 us
  waiting for transfers between devices  70.9 us (26%)
  blocking collectives  60.2 us (22%)
  matrix products  60 us (22%)
  local copies, waits for them, and re-layouts  41 us (15%)
  starting transfers between devices  19.2 us (7%)
  between operations  13.7 us (5%)
  other arithmetic  11.7 us (4%)
    all_to_all x1, blocking collectives, exchange_both(): lax.all_to_all(blocks, axis, split_axis=0, concat_axis=0, tiled=True)  60.2 us
    all_to_all x1, waiting for transfers between devices, exchange_both(): lax.all_to_all(blocks, axis, split_axis=0, concat_axis=0, tiled=True)  52.6 us
    dot_general x1, matrix products, shards(): jnp.einsum('nesf,efd->nesd', act, w_down, preferred_element_type=jnp.floa...  12.3 us
    all_to_all x1, waiting for transfers between devices, shards(): lax.all_to_all(attn, 'head', split_axis=0, concat_axis=1, tiled=True)  10.4 us
    dot_general x1, matrix products, shards(): projected = jnp.dot(all_heads, all_rows, preferred_element_type=jnp.float32)  9.08 us
    all_to_all x1, starting transfers between devices, shards(): lax.all_to_all(attn, 'head', split_axis=0, concat_axis=1, tiled=True)  9 us
    dot_general x4, matrix products, advance(): jnp.einsum('hid,hjd->hij', query_block, key_block, precision=HIGH) * lower  8.31 us
    dot_general x4, matrix products, advance(): jnp.einsum('hid,hde->hie', query_block, state, precision=HIGH)  8.17 us
  transfers between devices with their start and end apart: 6, of which 4 were waited for; matrix products, arithmetic and copies ran while one was open for 19% of the time, Pallas kernels for 0%

profile of v1, /device:TPU:1, one launch (start us, length us, event | category | flops | bytes accessed | tf_op | source)
XLA Modules:
  0.0 276.8 jit_solution(13803575728342648501)
XLA Ops:
  6.5 0.7 all-gather.2.cloned.1.call-update
  7.3 30.9 %while.13 = (s32[]{:T(128)}, f32[1,128,128]{2,1,0:T(8,128)S(1)}, f32[4,1,512,128]{3,2,1,0:T(8,128)}, f32[4,1,512,128]{3,2,1,0:T(8,128)}, f32[4,1,512,128]{3,2,1,...) while((s32[]{:T(128)}, f32[1,128,128]{2,1,0:T(8,128)S(1)}, ...), condition=%wide.region_1.2_spmd.clone, body=%wide.region_0.1_spmd.clone.sunk | while | flops 1007534080 | bytes 4656736 | solution.py:66
  7.3 2.2 convolution_multiply_fusion.2
  9.5 1.9 fusion.88
  11.5 2.0 fusion.89
  13.5 1.6 fusion.87
  15.2 2.0 convolution_multiply_fusion.2
  17.2 1.9 fusion.88
  19.1 2.0 fusion.89
  21.2 1.6 fusion.87
  22.9 2.1 convolution_multiply_fusion.2
  24.9 1.9 fusion.88
  26.9 2.0 fusion.89
  28.9 1.6 fusion.87
  30.6 2.0 convolution_multiply_fusion.2
  32.6 1.9 fusion.88
  34.6 2.0 fusion.89
  36.6 1.6 fusion.87
  38.2 0.6 convert_bitcast_fusion.1
  38.9 2.5 collective-permute-start
  41.4 2.0 collective-permute-start.2
  43.4 0.1 copy.29
  43.5 0.1 eq.32
  43.6 0.7 copy.31
  44.4 1.0 fusion.50
  45.5 0.7 broadcast_add_fusion
  46.2 0.1 eq.28
  46.3 2.9 %copy.37 = f32[2048,128]{0,1:T(8,128)} copy(f32[2048,128]{1,0:T(8,128)} %bitcast.187) | data formatting | bytes 2097152 | tf_op jit(solution)/shard_map/reshape;transpose | solution.py:69
  49.2 1.0 copy.32
  50.2 0.6 collective-permute-done.1
  50.8 0.8 constant_dynamic-update-slice_fusion.7
  51.5 0.8 constant_dynamic-update-slice_fusion.6
  52.3 0.8 constant_dynamic-update-slice_fusion.3
  53.1 0.8 constant_dynamic-update-slice_fusion.2
  53.9 0.1 multiply_reduce_fusion.2
  54.0 2.7 multiply_reduce_fusion
  56.7 0.9 multiply_convert_fusion
  57.5 2.1 copy.26
  59.6 9.0 %all-to-all-start = ((bf16[32,64,128]{2,1,0:T(8,128)(2,1)}), bf16[32,64,128]{2,1,0:T(8,128)(2,1)}, u32[]{:S(2)}, u32[]{:S(2)}) async-start(bf16[32,64,128]{2,1,0:T(8,128)(2,1)} %bitcast.185), calls=%async_computation | async-start | bytes 1048576 | tf_op jit(solution)/shard_map/all_to_all | solution.py:94
  68.6 0.2 fusion.49
  68.8 0.1 copy.28
  68.9 0.1 mul.78
  69.1 2.4 scatter_custom_fusion.1
  71.5 2.6 scatter_custom_fusion
  74.2 0.1 broadcast_in_dim.56
  74.3 10.4 %all-to-all-done = bf16[32,64,128]{2,1,0:T(8,128)(2,1)} async-done(((bf16[32,64,128]{2,1,0:T(8,128)(2,1)}), bf16[32,64,128]{2,1,0:T(8,128)(2,1)}, u32[]{:S(2)}, u32[]{:S(2)}) %all-to-all-start) | async-done | bytes 524320 | tf_op jit(solution)/shard_map/all_to_all | solution.py:94
  84.7 6.6 %all-gather.2.cloned.1.call-done = bf16[4096,2048]{1,0:T(8,128)(2,1)} async-done(((bf16[128,2048]{1,0:T(8,128)(2,1)}), bf16[4096,2048]{1,0:T(8,128)(2,1)}) %all-gather.2.cloned.1.call-update) | async-done | bytes 16777232 | tf_op jit(solution)/shard_map/all_gather | solution.py:95
  91.3 9.1 %multiply_reduce_fusion.1 = (f32[64]{0:T(128)S(1)}, f32[64,2048]{1,0:T(8,128)S(1)}) fusion(bf16[4096,2048]{1,0:T(8,128)(2,1)} %all-gather.2.cloned.1.call-done, bf16[32,64,128]{2,1,0:T(8,128)(2,1)} %all-to-all-done), kind=kOutput, calls=%fused_computation.59 | convolution fusion | flops 1074003968 | bytes 17826048 | tf_op jit(solution)/shard_map/dot_general | solution.py:96
  100.4 0.8 copy-done.1
  101.1 0.1 multiply_convert_fusion.1
  101.2 6.0 %gather_fusion = bf16[1024,2048]{1,0:T(8,128)(2,1)} fusion(bf16[64,2048]{1,0:T(8,128)(2,1)S(1)} %multiply_convert_fusion.1, s32[1024]{0:T(1024)S(1)} %fusion.54), kind=kCustom, calls=%fused_computation | custom fusion | bytes 8392704 | tf_op jit(solution)/shard_map/gather | solution.py:120
  107.3 2.5 bitcast_select_fusion
  109.8 60.2 %all_to_all.26 = bf16[128,1,1,1,8,2048]{5,4,3,2,1,0:T(8,128)(2,1)S(1)} all-to-all(bf16[128,1,1,1,8,2048]{5,4,3,2,1,0:T(8,128)(2,1)S(1)} %bitcast_select_fusion), channel_id=1, replica_groups=mesh['seq'=4,'head'=32] {'seq','head'}, dimensions={0} | all-to-all | bytes 8388608 | tf_op jit(solution)/shard_map/all_to_all | solution.py:42
  170.0 2.3 copy.34
  172.3 2.0 copy-done.2
  174.3 5.2 %fusion.30 = f32[128,8,768]{2,0,1:T(8,128)} fusion(bf16[128,8,2048]{2,0,1:T(8,128)(2,1)S(1)} %bitcast.183, bf16[1,2048,768]{2,1,0:T(8,128)(2,1)S(1)} %copy-done.5), kind=kOutput, calls=%fused_computation.41 | convolution fusion | flops 3221225472 | bytes 10485760 | tf_op jit(solution)/shard_map/nesd,edf->nesf/dot_general | solution.py:128
  179.5 12.3 %convert_bitcast_fusion = bf16[128,1,1,1,8,2048]{5,0,4,3,2,1:T(8,128)(2,1)} fusion(bf16[1,768,2048]{2,1,0:T(8,128)(2,1)S(1)} %copy-done, f32[128,8,768]{2,0,1:T(8,128)} %fusion.30, bf16[128,8,2048]{2,0,1:T(8,128)(2,1)} %bitcast.184, bf16[1,2048,768]{2,1,0:T(8,128)(2,1)} %param.17), kind=kOutput, calls=%fused_computation.37 | convolution fusion | flops 6449266688 | bytes 17825792 | tf_op jit(solution)/shard_map/nesf,efd->nesd/dot_general | solution.py:130
  191.8 6.5 %copy.35 = bf16[128,1,1,1,8,2048]{5,4,3,2,1,0:T(8,128)(2,1)} copy(bf16[128,1,1,1,8,2048]{5,0,4,3,2,1:T(8,128)(2,1)} %convert_bitcast_fusion) | data formatting | bytes 8388608 | tf_op jit(solution)/shard_map/reshape;transpose;transpose;reshape;reshape;reshape | solution.py:41
  198.3 5.6 %all-to-all-start.2 = ((bf16[128,1,1,1,8,2048]{5,4,3,2,1,0:T(8,128)(2,1)}), bf16[128,1,1,1,8,2048]{5,4,3,2,1,0:T(8,128)(2,1)}, u32[]{:S(2)}, u32[]{:S(2)}) async-start(bf16[128,1,1,1,8,2048]{5,4,3,2,1,0:T(8,128)(2,1)} %copy.35), calls=%async_computation.2 | async-start | bytes 8388608 | tf_op jit(solution)/shard_map/all_to_all | solution.py:42
  203.9 0.1 copy.36
  204.0 52.6 %all-to-all-done.2 = bf16[128,1,1,1,8,2048]{5,4,3,2,1,0:T(8,128)(2,1)} async-done(((bf16[128,1,1,1,8,2048]{5,4,3,2,1,0:T(8,128)(2,1)}), bf16[128,1,1,1,8,2048]{5,4,3,2,1,0:T(8,128)(2,1)}, u32[]{:S(2)}, u32[]{:S(2)}) %all-to-all-start.2) | async-done | bytes 4194336 | tf_op jit(solution)/shard_map/all_to_all | solution.py:42
  256.6 8.0 %gather_fusion.1 = bf16[512,2048]{1,0:T(8,128)(2,1)} fusion(bf16[1024,2048]{1,0:T(8,128)(2,1)} %bitcast.46, s32[1024]{0:T(1024)S(1)} %pad_clamp_fusion), kind=kCustom, calls=%fused_computation.1 | custom fusion | bytes 4196352 | tf_op jit(solution)/shard_map/gather | solution.py:136
  264.6 3.4 %fusion.27 = f32[64,2048]{1,0:T(8,128)S(1)} fusion(bf16[512,2048]{1,0:T(8,128)(2,1)} %gather_fusion.1, f32[64,8]{1,0:T(8,128)S(1)} %copy.36), kind=kLoop, calls=%fused_computation.35 | loop fusion | flops 3014656 | bytes 2623488 | tf_op jit(solution)/shard_map/reduce_sum | solution.py:137
  268.1 1.9 add.95
  (35 shorter events, 0.2 us)
Async XLA Ops:
  6.5 172.9 %copy-start = (bf16[1,768,2048]{2,1,0:T(8,128)(2,1)S(1)}, bf16[1,768,2048]{2,1,0:T(8,128)(2,1)}, u32[]{:S(2)}) copy-start(bf16[1,768,2048]{2,1,0:T(8,128)(2,1)} %param.19) | copy-start | bytes 9437188
  6.5 84.7 %all-gather.2.cloned.1.call-start = ((), (), s32[]{:S(2)}) async-start(), calls=%async_computation.3 | async-start | bytes 17301504 | tf_op jit(solution)/shard_map/all_gather | solution.py:95
  7.3 36.2 %copy-start.3 = (s32[64,8]{0,1:T(8,128)S(1)}, s32[64,8]{0,1:T(8,128)}, u32[]{:S(2)}) copy-start(s32[64,8]{0,1:T(8,128)} %param.15) | copy-start | bytes 6148
  38.9 7.3 %collective-permute-start = (bf16[1,1,128,128]{3,2,1,0:T(8,128)(2,1)}, bf16[1,1,128,128]{3,2,1,0:T(8,128)(2,1)}, u32[]{:S(2)}, u32[]{:S(2)}) collective-permute-start(bf16[1,1,128,128]{3,2,1,0:T(8,128)(2,1)} %convert_bitcast_fusion.1), channel_id=1, source_target_pairs={{0,32},{32,64},{64,96},{96,0},{1,33},{33,65},{65,97},{97,1},{2,34}... | collective-permute-start | bytes 98312 | tf_op jit(solution)/shard_map/ppermute | solution.py:17
  41.4 10.9 %collective-permute-start.2 = (bf16[1,1,128,128]{3,2,1,0:T(8,128)(2,1)}, bf16[1,1,128,128]{3,2,1,0:T(8,128)(2,1)S(1)}, u32[]{:S(2)}, u32[]{:S(2)}) collective-permute-start(bf16[1,1,128,128]{3,2,1,0:T(8,128)(2,1)} %convert_bitcast_fusion.1), channel_id=1, source_target_pairs={{0,96},{32,0},{64,32},{96,64},{1,97},{33,1},{65,33},{97,65},{2,98}... | collective-permute-start | bytes 98312 | tf_op jit(solution)/shard_map/ppermute | solution.py:19
  46.2 4.6 %collective-permute-start.1 = (bf16[1,1,128,128]{3,2,1,0:T(8,128)(2,1)}, bf16[1,1,128,128]{3,2,1,0:T(8,128)(2,1)}, u32[]{:S(2)}, u32[]{:S(2)}) collective-permute-start(bf16[1,1,128,128]{3,2,1,0:T(8,128)(2,1)} %collective-permute-done), channel_id=1, source_target_pairs={{0,32},{32,64},{64,96},{96,0},{1,33},{33,65},{65,97},{97,1},{2,34}... | collective-permute-start | bytes 98312 | tf_op jit(solution)/shard_map/ppermute | solution.py:17
  59.6 25.1 %all-to-all-start = ((bf16[32,64,128]{2,1,0:T(8,128)(2,1)}), bf16[32,64,128]{2,1,0:T(8,128)(2,1)}, u32[]{:S(2)}, u32[]{:S(2)}) async-start(bf16[32,64,128]{2,1,0:T(8,128)(2,1)} %bitcast.185), calls=%async_computation | async-start | bytes 1048576 | tf_op jit(solution)/shard_map/all_to_all | solution.py:94
  100.3 0.8 copy-start.1
  170.0 4.3 %copy-start.5 = (bf16[1,2048,768]{2,1,0:T(8,128)(2,1)S(1)}, bf16[1,2048,768]{2,1,0:T(8,128)(2,1)}, u32[]{:S(2)}) copy-start(bf16[1,2048,768]{2,1,0:T(8,128)(2,1)} %param.18) | copy-start | bytes 9437188
  172.3 2.0 copy-start.2
  198.2 5.6 %copy-start.4 = (s32[64,8]{0,1:T(8,128)S(1)}, s32[64,8]{0,1:T(8,128)}, u32[]{:S(2)}) copy-start(s32[64,8]{0,1:T(8,128)} %param.16) | copy-start | bytes 6148
  198.3 58.4 %all-to-all-start.2 = ((bf16[128,1,1,1,8,2048]{5,4,3,2,1,0:T(8,128)(2,1)}), bf16[128,1,1,1,8,2048]{5,4,3,2,1,0:T(8,128)(2,1)}, u32[]{:S(2)}, u32[]{:S(2)}) async-start(bf16[128,1,1,1,8,2048]{5,4,3,2,1,0:T(8,128)(2,1)} %copy.35), calls=%async_computation.2 | async-start | bytes 8388608 | tf_op jit(solution)/shard_map/all_to_all | solution.py:42
Sparse Core Ops, SparseCore 0:
  9.6 81.5 all-gather.1
